TPU v7x, 256 devices: a whole 4x4x8 slice. The times are simulated.
256 devices in a mesh: mem: 16 (over y_lo, x, core), tile: 16 (over y_hi, z).
Axes of the slice: x: 4, y: 4 (y_hi: 2, y_lo: 2; y = y_hi * 2 + y_lo), z: 8, core: 2. Of those that a mesh axis runs over, the one named last changes fastest.
Arguments:
- perturb: bfloat16 [80, 2, 2, 256, 2048], P('mem', None, None, None, 'tile'), may hold values from -6 to 6
- coef_x: float32 [2, 256, 2048], P(None, None, 'tile'), may hold values from 0.25 to 0.5
- coef_y: float32 [2, 256, 2048], P(None, None, 'tile'), may hold values from 0.25 to 0.5
- obs_values: float32 [524288], P(('mem', 'tile')), may hold values from -12 to 12
- obs_tile: int32 [524288, 1], P(('mem', 'tile')), may hold values from 0 to 15; in each aligned block of 2048 rows (0 to 2047, 2048 to 4095, ...) at most 384 rows name the same one
- obs_cell: int32 [524288], P(('mem', 'tile')), may hold values from 0 to 131071
Outputs:
- increment: float32 [256, 2, 2, 2048], P('mem', None, None, 'tile')
Inputs may be any that keep to these rules, and one draw needn't show every extreme that they name: `obs_tile`: among the 2048 observations of one device no tile is named more than 384 times, and in every draw some device names some tile exactly 384 times.
All inputs are finite; a program needn't handle non-finite values.
Results may differ from a plain program's by a relative error of at most 0.0003.
Values sent between devices are 32-bit elements; how exact they have to be, the bound alone decides.
A program may use at most 64 MiB of HBM per device.

v0:
```python
import jax
import jax.numpy as jnp
from jax import lax
from jax.sharding import PartitionSpec as P

FIELDS = 2
LEVELS = 2
SWEEPS = 6
LAT = 256


def extended_2(block, sides, width):
    for axis, dim in sides:
        count = lax.axis_size(axis)
        forward = [(i, i + 1) for i in range(count - 1)]
        forward.append((count - 1, 0))
        backward = [(target, source) for source, target in forward]
        low = lax.ppermute(
            lax.slice_in_dim(block, block.shape[dim] - width, None, axis=dim), axis, forward
        )
        high = lax.ppermute(lax.slice_in_dim(block, 0, width, axis=dim), axis, backward)
        block = jnp.concatenate([low, block, high], axis=dim)
    return block


def sweep_east(field, coef):
    flux = coef[..., :-1] * (field[..., 1:] - field[..., :-1])
    return field[..., 1:-1] + flux[..., 1:] - flux[..., :-1]


def sweep_north(field, coef):
    flux = coef[..., :-1, :] * (field[..., 1:, :] - field[..., :-1, :])
    zero_row = jnp.zeros(field.shape[:-2] + (1, field.shape[-1]), jnp.float32)
    upper = jnp.concatenate([flux, zero_row], axis=-2)
    lower = jnp.concatenate([zero_row, flux], axis=-2)
    return field + upper - lower


def deposit(lists, total_cells):
    cells = lists[1].astype(jnp.int32)
    return jnp.zeros((total_cells,), jnp.float32).at[cells].add(lists[0])


def on_device(perturb, coef_x, coef_y, obs_values, obs_tile, obs_cell):
    tiles = lax.axis_size("tile")
    members = perturb.shape[0] * lax.axis_size("mem")
    lon_local = perturb.shape[4]
    capacity = 3 * obs_values.shape[0] // tiles
    total_cells = FIELDS * LEVELS * LAT * lon_local
    target = obs_tile[:, 0]
    onehot = (jnp.arange(tiles, dtype=jnp.int32)[:, None] == target[None, :]).astype(jnp.int32)
    before = jnp.cumsum(onehot, axis=1) - onehot
    ranking = jnp.sum(before * onehot, axis=0)
    slot = target * capacity + ranking
    packed = jnp.stack([obs_values, obs_cell.astype(jnp.float32)])
    outgoing = jnp.zeros((2, tiles * capacity), jnp.float32).at[:, slot].set(packed)
    incoming = lax.all_to_all(outgoing, "tile", split_axis=1, concat_axis=1, tiled=True)
    adjoint_field = lax.psum(deposit(incoming, total_cells), "mem")
    adjoint_field = adjoint_field.reshape(FIELDS, LEVELS, LAT, lon_local)
    widened = perturb.astype(jnp.float32)
    product = jnp.sum(widened * adjoint_field[None], axis=1)
    joined = jnp.concatenate([product, coef_x[None]], axis=0)
    padded = extended_2(joined, (("tile", 3),), 1)
    coef_wide = padded[-1]
    product = sweep_east(padded[:-1], coef_wide)
    for step in range(SWEEPS - 1):
        extended = extended_2(product, (("tile", 3),), 1)
        product = sweep_east(extended, coef_wide)
    for step in range(SWEEPS):
        product = sweep_north(product, coef_y)
    summed = lax.psum_scatter(
        jnp.einsum("kflyx,klyx->yflx", widened, product), "mem", scatter_dimension=0, tiled=True
    )
    return summed / (members - 1)


def solution(mesh):
    return jax.shard_map(
        on_device,
        mesh=mesh,
        in_specs=(
            P("mem", None, None, None, "tile"),
            P(None, None, "tile"),
            P(None, None, "tile"),
            P(("mem", "tile")),
            P(("mem", "tile"), None),
            P(("mem", "tile")),
        ),
        out_specs=P("mem", None, None, "tile"),
        check_vma=False,
    )
```

profile of v0, /device:TPU:1, one launch (start us, length us, event | category | flops | bytes accessed | tf_op | source)
XLA Modules:
  0.0 436.6 jit_solution(9558857455044095042)
XLA Ops:
  7.2 4.5 %reduce-window.6 = s32[16,16,128]{2,1,0:T(8,128)S(1)} reduce-window(s32[16,16,128]{2,1,0:T(8,128)S(1)} %fusion.18, s32[]{:T(128)} %constant.8.clone.1), window={size=1x1x128 pad=0_0x0_0x127_0}, to_apply=%region_0.0 | reduce-window | flops 4161536 | bytes 262148 | tf_op jit(solution)/shard_map/reduce-window
  15.3 1.4 copy.13
  16.7 6.7 %scatter_custom_fusion = f32[2,6144]{0,1:T(8,128)S(1)} fusion(s32[2048]{0:T(1024)S(1)} %bitcast.52, f32[2048,2]{1,0:T(8,128)} %copy.13, f32[]{:T(128)} %constant.6.clone.1), kind=kCustom, calls=%fused_computation.22 | custom fusion | bytes 49664 | tf_op jit(solution)/shard_map/scatter | solution.py:56
  24.6 20.4 %all_to_all.9 = f32[2,16,384]{2,0,1:T(2,128)S(1)} all-to-all(f32[2,16,384]{2,0,1:T(2,128)S(1)} %copy.14), channel_id=1, replica_groups=mesh['mem'=16,'tile'=16] {'tile'}, dimensions={1} | all-to-all | bytes 98304 | tf_op jit(solution)/shard_map/all_to_all | solution.py:57
  45.1 41.9 %scatter_custom_fusion.1 = f32[131072]{0:T(1024)} fusion(s32[6144]{0:T(1024)S(1)} %bitcast.50, f32[6144]{0:T(1024)S(1)} %bitcast.51, f32[]{:T(128)} %constant.6.clone.1), kind=kCustom, calls=%fused_computation.59 | custom fusion | flops 6144 | bytes 524292 | tf_op jit(solution)/shard_map/scatter-add | solution.py:41
  87.1 118.6 %all-reduce.16.cloned.1.call-done = f32[2,2,256,128]{3,2,1,0:T(8,128)} async-done(((f32[2,2,256,128]{3,2,1,0:T(8,128)}), f32[2,2,256,128]{3,2,1,0:T(8,128)}) %all-reduce.16.cloned.1.call-update) | async-done | bytes 524304 | tf_op jit(solution)/shard_map/psum | solution.py:58
  205.7 1.9 multiply_reduce_fusion.1
  207.6 2.2 pad_maximum_fusion.4
  209.8 1.9 copy.15
  211.7 1.3 collective-permute-start
  213.0 1.9 copy.16
  214.9 4.0 collective-permute-start.1
  218.9 1.7 copy.17
  220.5 1.7 copy.18
  222.2 1.4 fusion.15
  225.4 1.5 fusion.23
  226.9 1.7 copy.21
  228.6 4.5 %collective-permute-start.2 = (f32[5,2,256,1]{2,1,3,0:T(2,128)S(1)}, f32[5,2,256,1]{2,1,3,0:T(2,128)S(1)}, u32[]{:S(2)}, u32[]{:S(2)}) collective-permute-start(f32[5,2,256,1]{2,1,3,0:T(2,128)S(1)} %copy.21), channel_id=1, source_target_pairs={{1,0},{2,1},{3,2},{4,3},{5,4},{6,5},{7,6},{8,7},{9,8},{10,9},{11,1... | collective-permute-start | bytes 30728 | tf_op jit(solution)/shard_map/ppermute | solution.py:21
  234.4 5.5 %collective-permute-done.3 = f32[5,2,256,1]{2,1,3,0:T(2,128)S(1)} collective-permute-done((f32[5,2,256,1]{2,1,3,0:T(2,128)S(1)}, f32[5,2,256,1]{2,1,3,0:T(2,128)S(1)}, u32[]{:S(2)}, u32[]{:S(2)}) %collective-permute-start.3) | collective-permute-done | bytes 10272 | tf_op jit(solution)/shard_map/ppermute | solution.py:18
  239.9 1.5 copy.24
  241.4 2.1 fusion.2
  243.9 1.5 fusion.22
  245.4 1.7 copy.25
  247.6 1.5 collective-permute-start.5
  250.1 3.6 collective-permute-done.5
  253.7 1.5 copy.28
  255.2 2.1 fusion.3
  257.7 1.5 fusion.21
  259.2 1.7 copy.29
  261.4 1.5 collective-permute-start.7
  263.9 3.6 collective-permute-done.7
  267.6 1.5 copy.32
  269.1 2.1 fusion.4
  271.6 1.5 fusion.20
  273.1 1.7 copy.33
  275.2 1.7 collective-permute-start.9
  277.8 3.8 collective-permute-done.9
  281.6 1.5 copy.36
  283.1 2.1 fusion.5
  285.6 1.5 fusion.19
  287.1 1.7 copy.37
  289.3 1.5 collective-permute-start.11
  291.8 3.6 collective-permute-done.11
  295.5 1.5 copy.40
  297.0 2.1 fusion.6
  303.6 1.2 copy.51
  306.1 122.3 %all-reduce.18.cloned.1.call-done = f32[256,2,2,128]{3,2,1,0:T(2,128)} async-done(((f32[256,2,2,128]{3,2,1,0:T(2,128)}), f32[256,2,2,128]{3,2,1,0:T(2,128)}) %all-reduce.18.cloned.1.call-update) | async-done | bytes 524304
  428.4 1.4 dynamic-slice_multiply_fusion
  (69 shorter events, 21.0 us)
Async XLA Ops:
  6.5 199.2 %all-reduce.16.cloned.1.call-start = ((), (), s32[]{:S(2)}) async-start(), calls=%async_computation.1 | async-start | bytes 1048576 | tf_op jit(solution)/shard_map/psum | solution.py:58
  87.0 120.6 %copy-start.4 = (f32[2,256,128]{2,1,0:T(8,128)S(1)}, f32[2,256,128]{2,1,0:T(8,128)}, u32[]{:S(2)}) copy-start(f32[2,256,128]{2,1,0:T(8,128)} %param.7) | copy-start | bytes 786436
  87.1 341.3 %all-reduce.18.cloned.1.call-start = ((), (), s32[]{:S(2)}) async-start(), calls=%async_computation.2 | async-start | bytes 1048576
  211.7 7.2 %collective-permute-start = (f32[6,2,256,1]{2,1,3,0:T(2,128)S(1)}, f32[6,2,256,1]{2,1,3,0:T(2,128)S(1)}, u32[]{:S(2)}, u32[]{:S(2)}) collective-permute-start(f32[6,2,256,1]{2,1,3,0:T(2,128)S(1)} %copy.15), channel_id=1, source_target_pairs={{0,1},{1,2},{2,3},{3,4},{4,5},{5,6},{6,7},{7,8},{8,9},{9,10},{10,1... | collective-permute-start | bytes 36872 | tf_op jit(solution)/shard_map/ppermute | solution.py:18
  214.9 5.7 %collective-permute-start.1 = (f32[6,2,256,1]{2,1,3,0:T(2,128)S(1)}, f32[6,2,256,1]{2,1,3,0:T(2,128)S(1)}, u32[]{:S(2)}, u32[]{:S(2)}) collective-permute-start(f32[6,2,256,1]{2,1,3,0:T(2,128)S(1)} %copy.16), channel_id=1, source_target_pairs={{1,0},{2,1},{3,2},{4,3},{5,4},{6,5},{7,6},{8,7},{9,8},{10,9},{11,1... | collective-permute-start | bytes 36872 | tf_op jit(solution)/shard_map/ppermute | solution.py:21
  222.2 1.6 copy-start
  222.2 2.0 copy-start.1
  228.6 5.3 %collective-permute-start.2 = (f32[5,2,256,1]{2,1,3,0:T(2,128)S(1)}, f32[5,2,256,1]{2,1,3,0:T(2,128)S(1)}, u32[]{:S(2)}, u32[]{:S(2)}) collective-permute-start(f32[5,2,256,1]{2,1,3,0:T(2,128)S(1)} %copy.21), channel_id=1, source_target_pairs={{1,0},{2,1},{3,2},{4,3},{5,4},{6,5},{7,6},{8,7},{9,8},{10,9},{11,1... | collective-permute-start | bytes 30728 | tf_op jit(solution)/shard_map/ppermute | solution.py:21
  233.5 6.4 %collective-permute-start.3 = (f32[5,2,256,1]{2,1,3,0:T(2,128)S(1)}, f32[5,2,256,1]{2,1,3,0:T(2,128)S(1)}, u32[]{:S(2)}, u32[]{:S(2)}) collective-permute-start(f32[5,2,256,1]{2,1,3,0:T(2,128)S(1)} %copy.23), channel_id=1, source_target_pairs={{0,1},{1,2},{2,3},{3,4},{4,5},{5,6},{6,7},{7,8},{8,9},{9,10},{10,1... | collective-permute-start | bytes 30728 | tf_op jit(solution)/shard_map/ppermute | solution.py:18
  247.1 2.6 collective-permute-start.4
  247.6 6.2 %collective-permute-start.5 = (f32[5,2,256,1]{2,1,3,0:T(2,128)S(1)}, f32[5,2,256,1]{2,1,3,0:T(2,128)S(1)}, u32[]{:S(2)}, u32[]{:S(2)}) collective-permute-start(f32[5,2,256,1]{2,1,3,0:T(2,128)S(1)} %copy.27), channel_id=1, source_target_pairs={{0,1},{1,2},{2,3},{3,4},{4,5},{5,6},{6,7},{7,8},{8,9},{9,10},{10,1... | collective-permute-start | bytes 30728 | tf_op jit(solution)/shard_map/ppermute | solution.py:18
  260.9 2.6 collective-permute-start.6
  261.4 6.2 %collective-permute-start.7 = (f32[5,2,256,1]{2,1,3,0:T(2,128)S(1)}, f32[5,2,256,1]{2,1,3,0:T(2,128)S(1)}, u32[]{:S(2)}, u32[]{:S(2)}) collective-permute-start(f32[5,2,256,1]{2,1,3,0:T(2,128)S(1)} %copy.31), channel_id=1, source_target_pairs={{0,1},{1,2},{2,3},{3,4},{4,5},{5,6},{6,7},{7,8},{8,9},{9,10},{10,1... | collective-permute-start | bytes 30728 | tf_op jit(solution)/shard_map/ppermute | solution.py:18
  274.8 2.6 collective-permute-start.8
  275.2 6.4 %collective-permute-start.9 = (f32[5,2,256,1]{2,1,3,0:T(2,128)S(1)}, f32[5,2,256,1]{2,1,3,0:T(2,128)S(1)}, u32[]{:S(2)}, u32[]{:S(2)}) collective-permute-start(f32[5,2,256,1]{2,1,3,0:T(2,128)S(1)} %copy.35), channel_id=1, source_target_pairs={{0,1},{1,2},{2,3},{3,4},{4,5},{5,6},{6,7},{7,8},{8,9},{9,10},{10,1... | collective-permute-start | bytes 30728 | tf_op jit(solution)/shard_map/ppermute | solution.py:18
  288.8 2.6 collective-permute-start.10
  289.3 6.2 %collective-permute-start.11 = (f32[5,2,256,1]{2,1,3,0:T(2,128)S(1)}, f32[5,2,256,1]{2,1,3,0:T(2,128)S(1)}, u32[]{:S(2)}, u32[]{:S(2)}) collective-permute-start(f32[5,2,256,1]{2,1,3,0:T(2,128)S(1)} %copy.39), channel_id=1, source_target_pairs={{0,1},{1,2},{2,3},{3,4},{4,5},{5,6},{6,7},{7,8},{8,9},{9,10},{10,1... | collective-permute-start | bytes 30728 | tf_op jit(solution)/shard_map/ppermute | solution.py:18
  299.0 1.0 copy-start.2
  302.0 1.3 copy-start.3
  303.6 1.2 copy-start.5
Sparse Core Ops, SparseCore 0:
  87.2 118.5 all-reduce.15
  305.0 123.3 all-reduce.17
where the time goes:
time: 438 us; the launch traced here: 437 us
  waiting for transfers between devices  264 us (60%)
  other arithmetic  73.1 us (17%)
  local copies, waits for them, and re-layouts  48.6 us (11%)
  blocking collectives  20.4 us (5%)
  starting transfers between devices  16.5 us (4%)
  between operations  14.4 us (3%)
    unnamed x3, waiting for transfers between devices  122 us
    psum x1, waiting for transfers between devices, on_device(): adjoint_field = lax.psum(deposit(incoming, total_cells), 'mem')  119 us
    scatter-add x1, other arithmetic, deposit(): return jnp.zeros((total_cells,), jnp.float32).at[cells].add(lists[0])  41.9 us
    all_to_all x1, blocking collectives, on_device(): lax.all_to_all(outgoing, 'tile', split_axis=1, concat_axis=1, tiled=True)  20.4 us
    ppermute x6, waiting for transfers between devices, extended_2(): lax.ppermute(lax.slice_in_dim(block, block.shape[dim] - width, None, axis...  20.2 us
    slice x11, local copies, waits for them, and re-layouts, extended_2(): lax.slice_in_dim(block, block.shape[dim] - width, None, axis=dim)  11.4 us
    mul x6, other arithmetic, sweep_east(): flux = coef[..., :-1] * (field[..., 1:] - field[..., :-1])  11 us
    slice x6, local copies, waits for them, and re-layouts, extended_2(): lax.slice_in_dim(block, 0, width, axis=dim)  10.4 us
  transfers between devices with their start and end apart: 14, of which 12 were waited for; matrix products, arithmetic and copies ran while one was open for 2% of the time, Pallas kernels for 0%

commit v1 on v0

--- a/solution.py
+++ b/solution.py
@@ -55,7 +55,7 @@
     packed = jnp.stack([obs_values, obs_cell.astype(jnp.float32)])
     outgoing = jnp.zeros((2, tiles * capacity), jnp.float32).at[:, slot].set(packed)
     incoming = lax.all_to_all(outgoing, "tile", split_axis=1, concat_axis=1, tiled=True)
-    adjoint_field = lax.psum(deposit(incoming, total_cells), "mem")
+    adjoint_field = jnp.sum(lax.all_gather(deposit(incoming, total_cells), "mem"), axis=0)
     adjoint_field = adjoint_field.reshape(FIELDS, LEVELS, LAT, lon_local)
     widened = perturb.astype(jnp.float32)
     product = jnp.sum(widened * adjoint_field[None], axis=1)

time: 438 us -> 382 us (0.87)
  waiting for transfers between devices: 264 us -> 198 us
  local copies, waits for them, and re-layouts: 48.6 us -> 55.3 us
    psum x1 -> x0, waiting for transfers between devices: 119 us -> none  [on_device(): adjoint_field = lax.psum(deposit(incoming, total_cells), 'mem')]
    all_gather x0 -> x1, waiting for transfers between devices: none -> 51.1 us  [on_device(): lax.all_gather(deposit(incoming, total_cells), 'mem')]
    all_gather x0 -> x1, local copies, waits for them, and re-layouts: none -> 6.16 us  [on_device(): lax.all_gather(deposit(incoming, total_cells), 'mem')]
    reduce_sum x0 -> x1, other arithmetic: none -> 4.86 us  [on_device(): jnp.sum(lax.all_gather(deposit(incoming, total_cells), 'mem'), axis=0)]
where the time goes in v1:
time: 382 us; the launch traced here: 381 us
  waiting for transfers between devices  198 us (52%)
  other arithmetic  76.5 us (20%)
  local copies, waits for them, and re-layouts  55.3 us (14%)
  blocking collectives  20.4 us (5%)
  starting transfers between devices  17 us (4%)
  between operations  14.4 us (4%)
    unnamed x3, waiting for transfers between devices  124 us
    all_gather x1, waiting for transfers between devices, on_device(): lax.all_gather(deposit(incoming, total_cells), 'mem')  51.1 us
    scatter-add x1, other arithmetic, deposit(): return jnp.zeros((total_cells,), jnp.float32).at[cells].add(lists[0])  42 us
    all_to_all x1, blocking collectives, on_device(): lax.all_to_all(outgoing, 'tile', split_axis=1, concat_axis=1, tiled=True)  20.4 us
    ppermute x6, waiting for transfers between devices, extended_2(): lax.ppermute(lax.slice_in_dim(block, block.shape[dim] - width, None, axis...  20.3 us
    slice x11, local copies, waits for them, and re-layouts, extended_2(): lax.slice_in_dim(block, block.shape[dim] - width, None, axis=dim)  11.3 us
    mul x6, other arithmetic, sweep_east(): flux = coef[..., :-1] * (field[..., 1:] - field[..., :-1])  11 us
    slice x6, local copies, waits for them, and re-layouts, extended_2(): lax.slice_in_dim(block, 0, width, axis=dim)  10.4 us
  transfers between devices with their start and end apart: 14, of which 12 were waited for; matrix products, arithmetic and copies ran while one was open for 2% of the time, Pallas kernels for 0%

profile of v1, /device:TPU:1, one launch (start us, length us, event | category | flops | bytes accessed | tf_op | source)
XLA Modules:
  0.0 381.3 jit_solution(4957496399833821157)
XLA Ops:
  7.2 4.5 %reduce-window.6 = s32[16,16,128]{2,1,0:T(8,128)S(1)} reduce-window(s32[16,16,128]{2,1,0:T(8,128)S(1)} %fusion.18, s32[]{:T(128)} %constant.8.clone.1), window={size=1x1x128 pad=0_0x0_0x127_0}, to_apply=%region_0.0 | reduce-window | flops 4161536 | bytes 262148 | tf_op jit(solution)/shard_map/reduce-window
  15.3 1.3 copy.41
  16.7 6.7 %scatter_custom_fusion = f32[2,6144]{0,1:T(8,128)S(1)} fusion(s32[2048]{0:T(1024)S(1)} %bitcast.52, f32[2048,2]{1,0:T(8,128)} %copy.41, f32[]{:T(128)} %constant.6.clone.1), kind=kCustom, calls=%fused_computation.22 | custom fusion | bytes 49664 | tf_op jit(solution)/shard_map/scatter | solution.py:56
  24.6 20.4 %all_to_all.9 = f32[2,16,384]{2,0,1:T(2,128)S(1)} all-to-all(f32[2,16,384]{2,0,1:T(2,128)S(1)} %copy.42), channel_id=1, replica_groups=mesh['mem'=16,'tile'=16] {'tile'}, dimensions={1} | all-to-all | bytes 98304 | tf_op jit(solution)/shard_map/all_to_all | solution.py:57
  45.1 42.0 %scatter_custom_fusion.1 = f32[131072]{0:T(1024)} fusion(s32[6144]{0:T(1024)S(1)} %bitcast.50, f32[6144]{0:T(1024)S(1)} %bitcast.51, f32[]{:T(128)} %constant.6.clone.1), kind=kCustom, calls=%fused_computation.59 | custom fusion | flops 6144 | bytes 524292 | tf_op jit(solution)/shard_map/scatter-add | solution.py:41
  87.1 51.1 %all-gather.3.cloned.1.call-done = f32[2097152]{0:T(1024)} async-done(((f32[131072]{0:T(1024)}), f32[2097152]{0:T(1024)}) %all-gather.3.cloned.1.call-update) | async-done | bytes 8388624 | tf_op jit(solution)/shard_map/all_gather | solution.py:58
  138.2 6.2 %reshape.74 = f32[16,131072]{1,0:T(8,128)} reshape(f32[2097152]{0:T(1024)} %all-gather.3.cloned.1.call-done) | data formatting | bytes 16777216 | tf_op jit(solution)/shard_map/all_gather | solution.py:58
  144.4 4.9 %reduce_sum.31 = f32[131072]{0:T(1024)S(1)} reduce(f32[16,131072]{1,0:T(8,128)} %reshape.74, f32[]{:T(128)} %constant.6.clone.1), dimensions={0}, to_apply=%region_5.6 | reduce | flops 1966080 | bytes 8912900 | tf_op jit(solution)/shard_map/reduce_sum | solution.py:58
  150.2 2.2 pad_maximum_fusion.4
  152.4 1.9 copy.43
  154.3 1.3 collective-permute-start
  155.6 1.9 copy.44
  157.5 4.3 %collective-permute-start.1 = (f32[6,2,256,1]{2,1,3,0:T(2,128)S(1)}, f32[6,2,256,1]{2,1,3,0:T(2,128)S(1)}, u32[]{:S(2)}, u32[]{:S(2)}) collective-permute-start(f32[6,2,256,1]{2,1,3,0:T(2,128)S(1)} %copy.44), channel_id=1, source_target_pairs={{1,0},{2,1},{3,2},{4,3},{5,4},{6,5},{7,6},{8,7},{9,8},{10,9},{11,1... | collective-permute-start | bytes 36872 | tf_op jit(solution)/shard_map/ppermute | solution.py:21
  161.8 1.7 copy.45
  163.5 1.7 copy.46
  165.2 1.4 fusion.15
  168.4 1.5 fusion.23
  169.9 1.7 copy.49
  171.6 4.5 %collective-permute-start.2 = (f32[5,2,256,1]{2,1,3,0:T(2,128)S(1)}, f32[5,2,256,1]{2,1,3,0:T(2,128)S(1)}, u32[]{:S(2)}, u32[]{:S(2)}) collective-permute-start(f32[5,2,256,1]{2,1,3,0:T(2,128)S(1)} %copy.49), channel_id=1, source_target_pairs={{1,0},{2,1},{3,2},{4,3},{5,4},{6,5},{7,6},{8,7},{9,8},{10,9},{11,1... | collective-permute-start | bytes 30728 | tf_op jit(solution)/shard_map/ppermute | solution.py:21
  177.4 5.3 %collective-permute-done.3 = f32[5,2,256,1]{2,1,3,0:T(2,128)S(1)} collective-permute-done((f32[5,2,256,1]{2,1,3,0:T(2,128)S(1)}, f32[5,2,256,1]{2,1,3,0:T(2,128)S(1)}, u32[]{:S(2)}, u32[]{:S(2)}) %collective-permute-start.3) | collective-permute-done | bytes 10272 | tf_op jit(solution)/shard_map/ppermute | solution.py:18
  182.7 1.5 copy.52
  184.2 2.1 fusion.2
  186.7 1.5 fusion.22
  188.2 1.7 copy.53
  190.3 1.5 collective-permute-start.5
  192.9 3.6 collective-permute-done.5
  196.5 1.5 copy.56
  198.0 2.1 fusion.3
  200.5 1.5 fusion.21
  202.0 1.7 copy.57
  204.2 1.7 collective-permute-start.7
  206.7 3.8 %collective-permute-done.7 = f32[5,2,256,1]{2,1,3,0:T(2,128)S(1)} collective-permute-done((f32[5,2,256,1]{2,1,3,0:T(2,128)S(1)}, f32[5,2,256,1]{2,1,3,0:T(2,128)S(1)}, u32[]{:S(2)}, u32[]{:S(2)}) %collective-permute-start.7) | collective-permute-done | bytes 10272 | tf_op jit(solution)/shard_map/ppermute | solution.py:18
  210.6 1.5 copy.60
  212.1 2.1 fusion.4
  214.6 1.5 fusion.20
  216.1 1.7 copy.61
  218.2 1.5 collective-permute-start.9
  220.8 3.6 collective-permute-done.9
  224.4 1.5 copy.64
  225.9 2.1 fusion.5
  228.4 1.5 fusion.19
  229.9 1.7 copy.65
  232.0 1.8 collective-permute-start.11
  234.6 3.9 %collective-permute-done.11 = f32[5,2,256,1]{2,1,3,0:T(2,128)S(1)} collective-permute-done((f32[5,2,256,1]{2,1,3,0:T(2,128)S(1)}, f32[5,2,256,1]{2,1,3,0:T(2,128)S(1)}, u32[]{:S(2)}, u32[]{:S(2)}) %collective-permute-start.11) | collective-permute-done | bytes 10272 | tf_op jit(solution)/shard_map/ppermute | solution.py:18
  238.5 1.5 copy.68
  240.0 2.1 fusion.6
  249.1 124.0 %all-reduce.15.cloned.1.call-done = f32[256,2,2,128]{3,2,1,0:T(2,128)} async-done(((f32[256,2,2,128]{3,2,1,0:T(2,128)}), f32[256,2,2,128]{3,2,1,0:T(2,128)}) %all-reduce.15.cloned.1.call-update) | async-done | bytes 524304
  373.1 1.4 dynamic-slice_multiply_fusion
  (73 shorter events, 22.9 us)
Async XLA Ops:
  6.5 131.7 %all-gather.3.cloned.1.call-start = ((), (), s32[]{:S(2)}) async-start(), calls=%async_computation.1 | async-start | bytes 8912896 | tf_op jit(solution)/shard_map/all_gather | solution.py:58
  87.1 286.0 %all-reduce.15.cloned.1.call-start = ((), (), s32[]{:S(2)}) async-start(), calls=%async_computation.2 | async-start | bytes 1048576
  144.4 4.9 %copy-start.3 = (bf16[5,2,2,256,128]{4,3,2,1,0:T(8,128)(2,1)S(1)}, bf16[5,2,2,256,128]{4,3,2,1,0:T(8,128)(2,1)}, u32[]{:S(2)}) copy-start(bf16[5,2,2,256,128]{4,3,2,1,0:T(8,128)(2,1)} %param.6) | copy-start | bytes 3932164
  149.3 1.0 copy-start.5
  154.3 7.5 %collective-permute-start = (f32[6,2,256,1]{2,1,3,0:T(2,128)S(1)}, f32[6,2,256,1]{2,1,3,0:T(2,128)S(1)}, u32[]{:S(2)}, u32[]{:S(2)}) collective-permute-start(f32[6,2,256,1]{2,1,3,0:T(2,128)S(1)} %copy.43), channel_id=1, source_target_pairs={{0,1},{1,2},{2,3},{3,4},{4,5},{5,6},{6,7},{7,8},{8,9},{9,10},{10,1... | collective-permute-start | bytes 36872 | tf_op jit(solution)/shard_map/ppermute | solution.py:18
  157.5 6.0 %collective-permute-start.1 = (f32[6,2,256,1]{2,1,3,0:T(2,128)S(1)}, f32[6,2,256,1]{2,1,3,0:T(2,128)S(1)}, u32[]{:S(2)}, u32[]{:S(2)}) collective-permute-start(f32[6,2,256,1]{2,1,3,0:T(2,128)S(1)} %copy.44), channel_id=1, source_target_pairs={{1,0},{2,1},{3,2},{4,3},{5,4},{6,5},{7,6},{8,7},{9,8},{10,9},{11,1... | collective-permute-start | bytes 36872 | tf_op jit(solution)/shard_map/ppermute | solution.py:21
  165.2 1.6 copy-start
  165.2 2.0 copy-start.1
  171.6 5.3 %collective-permute-start.2 = (f32[5,2,256,1]{2,1,3,0:T(2,128)S(1)}, f32[5,2,256,1]{2,1,3,0:T(2,128)S(1)}, u32[]{:S(2)}, u32[]{:S(2)}) collective-permute-start(f32[5,2,256,1]{2,1,3,0:T(2,128)S(1)} %copy.49), channel_id=1, source_target_pairs={{1,0},{2,1},{3,2},{4,3},{5,4},{6,5},{7,6},{8,7},{9,8},{10,9},{11,1... | collective-permute-start | bytes 30728 | tf_op jit(solution)/shard_map/ppermute | solution.py:21
  176.5 6.2 %collective-permute-start.3 = (f32[5,2,256,1]{2,1,3,0:T(2,128)S(1)}, f32[5,2,256,1]{2,1,3,0:T(2,128)S(1)}, u32[]{:S(2)}, u32[]{:S(2)}) collective-permute-start(f32[5,2,256,1]{2,1,3,0:T(2,128)S(1)} %copy.51), channel_id=1, source_target_pairs={{0,1},{1,2},{2,3},{3,4},{4,5},{5,6},{6,7},{7,8},{8,9},{9,10},{10,1... | collective-permute-start | bytes 30728 | tf_op jit(solution)/shard_map/ppermute | solution.py:18
  189.9 2.6 collective-permute-start.4
  190.3 6.2 %collective-permute-start.5 = (f32[5,2,256,1]{2,1,3,0:T(2,128)S(1)}, f32[5,2,256,1]{2,1,3,0:T(2,128)S(1)}, u32[]{:S(2)}, u32[]{:S(2)}) collective-permute-start(f32[5,2,256,1]{2,1,3,0:T(2,128)S(1)} %copy.55), channel_id=1, source_target_pairs={{0,1},{1,2},{2,3},{3,4},{4,5},{5,6},{6,7},{7,8},{8,9},{9,10},{10,1... | collective-permute-start | bytes 30728 | tf_op jit(solution)/shard_map/ppermute | solution.py:18
  203.7 2.6 collective-permute-start.6
  204.2 6.4 %collective-permute-start.7 = (f32[5,2,256,1]{2,1,3,0:T(2,128)S(1)}, f32[5,2,256,1]{2,1,3,0:T(2,128)S(1)}, u32[]{:S(2)}, u32[]{:S(2)}) collective-permute-start(f32[5,2,256,1]{2,1,3,0:T(2,128)S(1)} %copy.59), channel_id=1, source_target_pairs={{0,1},{1,2},{2,3},{3,4},{4,5},{5,6},{6,7},{7,8},{8,9},{9,10},{10,1... | collective-permute-start | bytes 30728 | tf_op jit(solution)/shard_map/ppermute | solution.py:18
  217.8 2.6 collective-permute-start.8
  218.2 6.2 %collective-permute-start.9 = (f32[5,2,256,1]{2,1,3,0:T(2,128)S(1)}, f32[5,2,256,1]{2,1,3,0:T(2,128)S(1)}, u32[]{:S(2)}, u32[]{:S(2)}) collective-permute-start(f32[5,2,256,1]{2,1,3,0:T(2,128)S(1)} %copy.63), channel_id=1, source_target_pairs={{0,1},{1,2},{2,3},{3,4},{4,5},{5,6},{6,7},{7,8},{8,9},{9,10},{10,1... | collective-permute-start | bytes 30728 | tf_op jit(solution)/shard_map/ppermute | solution.py:18
  231.6 2.6 collective-permute-start.10
  232.0 6.4 %collective-permute-start.11 = (f32[5,2,256,1]{2,1,3,0:T(2,128)S(1)}, f32[5,2,256,1]{2,1,3,0:T(2,128)S(1)}, u32[]{:S(2)}, u32[]{:S(2)}) collective-permute-start(f32[5,2,256,1]{2,1,3,0:T(2,128)S(1)} %copy.67), channel_id=1, source_target_pairs={{0,1},{1,2},{2,3},{3,4},{4,5},{5,6},{6,7},{7,8},{8,9},{9,10},{10,1... | collective-permute-start | bytes 30728 | tf_op jit(solution)/shard_map/ppermute | solution.py:18
  242.1 1.0 copy-start.2
  245.1 1.3 copy-start.4
  246.7 1.2 copy-start.6
Sparse Core Ops, SparseCore 0:
  87.2 50.9 all-gather.2
  248.0 125.0 all-reduce.14
